TPU v7x, 256 devices: a whole 4x4x8 slice. The times are simulated.
256 devices in a mesh: src: 16 (over z, x_hi), tgt: 16 (over x_lo, y, core).
Axes of the slice: x: 4 (x_hi: 2, x_lo: 2; x = x_hi * 2 + x_lo), y: 4, z: 8, core: 2. Of those that a mesh axis runs over, the one named last changes fastest.
Arguments:
- src_emb: bfloat16 [64, 32768], P(None, 'src'), may hold values from -2.75 to 2.75
- tgt_emb: bfloat16 [64, 131072], P(None, 'tgt'), may hold values from -2.75 to 2.75
- target_features: bfloat16 [128, 131072], P(None, 'tgt'), may hold values from -6 to 6
- src_mass: float32 [32768], P('src'), may hold values from 1 to 10
- tgt_mass: float32 [131072], P('tgt'), may hold values from 1 to 10
- kept_blocks: int32 [128, 128], P('src', 'tgt'), may hold values from 0 to 31, as said below
- kept_count: int32 [128, 16], P('src', 'tgt'), may hold values from 1 to 8
Outputs:
- projected: float32 [32768, 128], P(('src', 'tgt'))
- src_potential: float32 [32768], P('src')
- tgt_potential: float32 [131072], P('tgt')
Inputs may be any that keep to these rules, and one draw needn't show every extreme that they name: `kept_blocks`: entry [r, t * 8 + k] is a block number within target shard t; the 8 entries of one group are distinct; the first kept_count[r, t] of them are kept, the others are unused; every target block is kept by some source block row.
All inputs are finite; a program needn't handle non-finite values.
Results may differ from a plain program's by a relative error of at most 0.00075.
Values sent between devices are 32-bit elements; how exact they have to be, the bound alone decides.
A program may use at most 64 MiB of HBM per device.

v0:
```python
import jax
import jax.numpy as jnp
from jax import lax
from jax.sharding import PartitionSpec as P

BLOCK = 256
ITERS = 2
SENTINEL = -1e30
EPSILON = 0.1


def pair_distance(src_tile, norm_tile, tgt_chosen, tgt_norm_chosen):
    products = jnp.einsum("dr,dkc->krc", src_tile, tgt_chosen, preferred_element_type=jnp.float32)
    return norm_tile[None, :, None] + tgt_norm_chosen[:, None, :] - 2.0 * products


def merge_rows(highest, totals):
    overall = lax.pmax(highest, "tgt")
    return (overall, lax.psum(totals * jnp.exp(highest - overall), "tgt"))


def merge_columns(block_top, block_sum):
    overall = lax.pmax(block_top, "src")
    return (overall, lax.psum(block_sum * jnp.exp(block_top - overall), "src"))


def shards(src_emb, tgt_emb, target_features, src_mass, tgt_mass, kept_blocks, kept_count):
    emb_width = src_emb.shape[0]
    src_rows = src_emb.shape[1]
    tgt_rows = tgt_emb.shape[1]
    src_blocks = src_rows // BLOCK
    tgt_blocks = tgt_rows // BLOCK
    slot_count = kept_blocks.shape[1]
    src_tiles = src_emb.reshape(emb_width, src_blocks, BLOCK).transpose(1, 0, 2)
    src_norm = jnp.sum(jnp.square(src_emb.astype(jnp.float32)), axis=0).reshape(src_blocks, BLOCK)
    tgt_tiles = tgt_emb.reshape(emb_width, tgt_blocks, BLOCK)
    target_norm = jnp.sum(jnp.square(tgt_emb.astype(jnp.float32)), axis=0).reshape(
        tgt_blocks, BLOCK
    )
    feat_tiles = target_features.reshape(target_features.shape[0], tgt_blocks, BLOCK)
    live_slot = lax.broadcasted_iota(jnp.int32, (src_blocks, slot_count), 1) < kept_count
    packets = (src_tiles, src_norm, kept_blocks, live_slot)
    flat_index = kept_blocks.reshape(-1)
    member = (
        lax.broadcasted_iota(jnp.int32, (tgt_blocks, flat_index.shape[0]), 0) == flat_index[None, :]
    )

    def distances(packet):
        return pair_distance(
            packet[0],
            packet[1],
            jnp.take(tgt_tiles, packet[2], axis=1),
            jnp.take(target_norm, packet[2], axis=0),
        )

    def row_scaled(potential_tiles, packet):
        scaled = (
            jnp.take(potential_tiles, packet[2], axis=0)[:, None, :] - distances(packet)
        ) / EPSILON
        return jnp.where(packet[3][:, None, None], scaled, SENTINEL)

    tgt_potential = jnp.zeros((tgt_rows,), jnp.float32)
    src_potential = jnp.zeros((src_rows,), jnp.float32)
    for iteration in range(ITERS):
        row_potential_tiles = tgt_potential.reshape(tgt_blocks, BLOCK)

        def row_per_block(packet):
            scaled = row_scaled(row_potential_tiles, packet)
            highest = jnp.max(scaled, axis=(0, 2))
            totals = jnp.sum(
                jnp.where(packet[3][:, None, None], jnp.exp(scaled - highest[None, :, None]), 0.0),
                axis=(0, 2),
            )
            return (highest, totals)

        highest, totals = lax.map(row_per_block, packets)
        highest, totals = merge_rows(*(highest.reshape(src_rows), totals.reshape(src_rows)))
        src_potential = EPSILON * jnp.log(src_mass) - EPSILON * (highest + jnp.log(totals))
        column_potential_tiles = src_potential.reshape(src_blocks, BLOCK)

        def column_per_block(packet):
            scaled = (packet[4][None, :, None] - distances(packet)) / EPSILON
            scaled = jnp.where(packet[3][:, None, None], scaled, SENTINEL)
            highest = jnp.max(scaled, axis=1)
            totals = jnp.sum(
                jnp.where(packet[3][:, None, None], jnp.exp(scaled - highest[:, None, :]), 0.0),
                axis=1,
            )
            return (highest, totals)

        slot_top, slot_sum = lax.map(column_per_block, packets + (column_potential_tiles,))
        slot_top = slot_top.reshape(src_blocks * slot_count, BLOCK)
        slot_sum = slot_sum.reshape(src_blocks * slot_count, BLOCK)
        block_top = jnp.max(jnp.where(member[:, :, None], slot_top[None, :, :], SENTINEL), axis=1)
        scaled_sum = slot_sum * jnp.exp(slot_top - jnp.take(block_top, flat_index, axis=0))
        block_sum = jnp.dot(member.astype(jnp.float32), scaled_sum, precision=lax.Precision.HIGHEST)
        block_top, block_sum = merge_columns(
            *(block_top.reshape(tgt_rows), block_sum.reshape(tgt_rows))
        )
        tgt_potential = EPSILON * jnp.log(tgt_mass) - EPSILON * (block_top + jnp.log(block_sum))
    final_tiles = tgt_potential.reshape(tgt_blocks, BLOCK)

    def local_peak(packet):
        return jnp.max(row_scaled(final_tiles, packet), axis=(0, 2))

    local_top = lax.map(local_peak, packets)

    def weigh(packet):
        scaled = row_scaled(final_tiles, packet)
        weights = jnp.where(
            packet[3][:, None, None], jnp.exp(scaled - packet[4][None, :, None]), 0.0
        )
        rounded_count = lax.optimization_barrier(weights.astype(jnp.bfloat16))
        numerator = jnp.einsum(
            "krc,fkc->rf",
            rounded_count,
            jnp.take(feat_tiles, packet[2], axis=1),
            preferred_element_type=jnp.float32,
        )
        return (numerator, jnp.sum(rounded_count.astype(jnp.float32), axis=(0, 2)))

    numerator, denominator = lax.map(weigh, packets + (local_top,))
    numerator = numerator.reshape(src_rows, target_features.shape[0])
    denominator = denominator.reshape(src_rows)
    local_top = local_top.reshape(src_rows)
    share_rows = src_rows // lax.axis_size("tgt")
    first_row = lax.axis_index("tgt") * share_rows
    overall = lax.pmax(local_top, "tgt")
    factor = jnp.exp(local_top - overall)
    numerator = numerator * factor[:, None]
    denominator = denominator * factor
    numerator, denominator = lax.psum((numerator, denominator), "tgt")
    numerator = lax.dynamic_slice_in_dim(numerator, first_row, share_rows, 0)
    denominator = lax.dynamic_slice_in_dim(denominator, first_row, share_rows, 0)
    projected = numerator / denominator[:, None]
    return (projected, src_potential, tgt_potential)


def solution(mesh):
    return jax.shard_map(
        shards,
        mesh=mesh,
        in_specs=(
            P(None, "src"),
            P(None, "tgt"),
            P(None, "tgt"),
            P("src"),
            P("tgt"),
            P("src", "tgt"),
            P("src", "tgt"),
        ),
        out_specs=(P(("src", "tgt"), None), P("src"), P("tgt")),
        check_vma=False,
    )
```

profile of v0, /device:TPU:1, one launch (start us, length us, event | category | flops | bytes accessed | tf_op | source)
XLA Modules:
  0.0 761.6 jit_solution(7564907167131679846)
XLA Ops:
  11.3 26.2 %while.70 = (s32[]{:T(128)}, f32[8,256]{1,0:T(8,128)S(1)}, f32[8,256]{1,0:T(8,128)S(1)}, pred[8,8]{1,0:T(8,128)(4,1)S(1)}, s32[8,8]{1,0:T(8,128)S(1)}, /*index=5...) while((s32[]{:T(128)}, f32[8,256]{1,0:T(8,128)S(1)}, ...), condition=%wide.region_5.8_spmd, body=%wide.region_2.7_spmd.sunk | while | flops 72487472 | bytes 5143929 | solution.py:76
  37.5 30.2 %pmax.35 = f32[2048]{0:T(1024)S(1)} all-reduce(f32[2048]{0:T(1024)S(1)} %bitcast.348), channel_id=1, replica_groups=mesh['src'=16,'tgt'=16] {'tgt'}, use_global_device_ids=true, to_apply=%region_6.9 | all-reduce | flops 2048 | bytes 16384 | tf_op jit(solution)/shard_map/pmax | solution.py:18
  67.8 29.3 %psum.42 = f32[2048]{0:T(1024)S(1)} all-reduce(f32[2048]{0:T(1024)S(1)} %exponential_multiply_fusion.3), channel_id=1, replica_groups=mesh['src'=16,'tgt'=16] {'tgt'}, use_global_device_ids=true, to_apply=%region_7.10 | all-reduce | flops 2048 | bytes 16384 | tf_op jit(solution)/shard_map/psum | solution.py:19
  97.1 19.6 %while.71 = (s32[]{:T(128)}, f32[8,8,256]{2,1,0:T(8,128)S(1)}, f32[8,8,256]{2,1,0:T(8,128)S(1)}, pred[8,8]{1,0:T(8,128)(4,1)S(1)}, f32[8,256]{1,0:T(8,128)S(1)},...) while((s32[]{:T(128)}, f32[8,8,256]{2,1,0:T(8,128)S(1)}, ...), condition=%wide.region_11.14_spmd, body=%wide.region_8.13_spmd.sunk | while | flops 72481840 | bytes 5123405 | solution.py:91
  118.2 66.0 %pmax.36 = f32[8192]{0:T(1024)S(1)} all-reduce(f32[8192]{0:T(1024)S(1)} %bitcast.335), channel_id=1, replica_groups=mesh['src'=16,'tgt'=16] {'src'}, use_global_device_ids=true, to_apply=%region_13.16 | all-reduce | flops 8192 | bytes 65536 | tf_op jit(solution)/shard_map/pmax | solution.py:23
  184.3 58.0 %psum.43 = f32[8192]{0:T(1024)S(1)} all-reduce(f32[8192]{0:T(1024)S(1)} %exponential_multiply_fusion.1), channel_id=1, replica_groups=mesh['src'=16,'tgt'=16] {'src'}, use_global_device_ids=true, to_apply=%region_14.18 | all-reduce | flops 8192 | bytes 65536 | tf_op jit(solution)/shard_map/psum | solution.py:24
  242.3 26.1 %while.72 = (s32[]{:T(128)}, f32[8,256]{1,0:T(8,128)S(1)}, f32[8,256]{1,0:T(8,128)S(1)}, pred[8,8]{1,0:T(8,128)(4,1)S(1)}, s32[8,8]{1,0:T(8,128)S(1)}, /*index=5...) while((s32[]{:T(128)}, f32[8,256]{1,0:T(8,128)S(1)}, ...), condition=%wide.region_18.22_spmd, body=%wide.region_15.21_spmd.sunk | while | flops 72487472 | bytes 5111157 | solution.py:76
  268.5 55.3 %pmax.37 = f32[2048]{0:T(1024)S(1)} all-reduce(f32[2048]{0:T(1024)S(1)} %bitcast.350), channel_id=1, replica_groups=mesh['src'=16,'tgt'=16] {'tgt'}, use_global_device_ids=true, to_apply=%region_19.23 | all-reduce | flops 2048 | bytes 16384 | tf_op jit(solution)/shard_map/pmax | solution.py:18
  323.8 27.6 %psum.44 = f32[2048]{0:T(1024)S(1)} all-reduce(f32[2048]{0:T(1024)S(1)} %exponential_multiply_fusion.2), channel_id=1, replica_groups=mesh['src'=16,'tgt'=16] {'tgt'}, use_global_device_ids=true, to_apply=%region_20.24 | all-reduce | flops 2048 | bytes 16384 | tf_op jit(solution)/shard_map/psum | solution.py:19
  352.1 19.6 %while.73 = (s32[]{:T(128)}, f32[8,8,256]{2,1,0:T(8,128)S(1)}, f32[8,8,256]{2,1,0:T(8,128)S(1)}, pred[8,8]{1,0:T(8,128)(4,1)S(1)}, f32[8,256]{1,0:T(8,128)S(1)},...) while((s32[]{:T(128)}, f32[8,8,256]{2,1,0:T(8,128)S(1)}, ...), condition=%wide.region_24.28_spmd, body=%wide.region_21.27_spmd.sunk | while | flops 72481840 | bytes 5123405 | solution.py:91
  373.1 59.6 %pmax.38 = f32[8192]{0:T(1024)S(1)} all-reduce(f32[8192]{0:T(1024)S(1)} %bitcast.337), channel_id=1, replica_groups=mesh['src'=16,'tgt'=16] {'src'}, use_global_device_ids=true, to_apply=%region_26.30 | all-reduce | flops 8192 | bytes 65536 | tf_op jit(solution)/shard_map/pmax | solution.py:23
  432.8 58.6 %psum.45 = f32[8192]{0:T(1024)S(1)} all-reduce(f32[8192]{0:T(1024)S(1)} %exponential_multiply_fusion), channel_id=1, replica_groups=mesh['src'=16,'tgt'=16] {'src'}, use_global_device_ids=true, to_apply=%region_27.31 | all-reduce | flops 8192 | bytes 65536 | tf_op jit(solution)/shard_map/psum | solution.py:24
  492.0 24.2 %while.74 = (s32[]{:T(128)}, f32[8,256]{1,0:T(8,128)S(1)}, pred[8,8]{1,0:T(8,128)(4,1)S(1)}, s32[8,8]{1,0:T(8,128)S(1)}, f32[32,256]{1,0:T(8,128)S(1)}, /*index=...) while((s32[]{:T(128)}, f32[8,256]{1,0:T(8,128)S(1)}, ...), condition=%wide.region_30.34_spmd, body=%wide.region_28.33_spmd.sunk | while | flops 70914864 | bytes 912737 | solution.py:106
  516.2 3.2 copy.51
  519.4 2.9 copy.54
  522.4 55.7 %while.75 = (s32[]{:T(128)}, f32[8,256,128]{2,1,0:T(8,128)}, f32[8,256]{1,0:T(8,128)S(1)}, pred[8,8]{1,0:T(8,128)(4,1)S(1)}, s32[8,8]{1,0:T(8,128)S(1)}, /*index...) while((s32[]{:T(128)}, f32[8,256,128]{2,1,0:T(8,128)}, ...), condition=%wide.region_33.37_spmd, body=%wide.region_31.36_spmd.sunk | while | flops 207492928 | bytes 5770245 | solution.py:122
  525.6 2.2 gather_fusion.16
  539.6 2.2 gather_fusion.16
  546.5 2.2 gather_fusion.16
  574.4 2.2 gather_fusion.16
  578.1 54.6 %pmax.39 = f32[2048]{0:T(1024)S(1)} all-reduce(f32[2048]{0:T(1024)S(1)} %bitcast.346), channel_id=1, replica_groups=mesh['src'=16,'tgt'=16] {'tgt'}, use_global_device_ids=true, to_apply=%region_34.38 | all-reduce | flops 2048 | bytes 16384 | tf_op jit(solution)/shard_map/pmax | solution.py:128
  632.8 2.6 bitcast_multiply_fusion
  635.4 27.6 %psum.47 = f32[2048]{0:T(1024)S(1)} all-reduce(f32[2048]{0:T(1024)S(1)} %get-tuple-element.646), channel_id=1, replica_groups=mesh['src'=16,'tgt'=16] {'tgt'}, use_global_device_ids=true, to_apply=%region_36.40 | all-reduce | flops 2048 | bytes 16384 | tf_op jit(solution)/shard_map/psum | solution.py:132
  663.1 90.1 %all-reduce.2.cloned.1.call-done = f32[2048,128]{1,0:T(8,128)} async-done(((f32[2048,128]{1,0:T(8,128)}), f32[2048,128]{1,0:T(8,128)}) %all-reduce.2.cloned.1.call-update) | async-done | bytes 1048592 | tf_op jit(solution)/shard_map/psum | solution.py:132
  (643 shorter events, 168.9 us)
Async XLA Ops:
  7.2 3.8 copy-start
  7.2 746.0 %all-reduce.2.cloned.1.call-start = ((), (), s32[]{:S(2)}) async-start(), calls=%async_computation | async-start | bytes 2097152 | tf_op jit(solution)/shard_map/psum | solution.py:132
  8.1 3.1 copy-start.6
  8.1 3.2 copy-start.3
  11.3 85.8 %copy-start.5 = (f32[2048]{0:T(1024)S(1)}, f32[2048]{0:T(1024)}, u32[]{:S(2)}) copy-start(f32[2048]{0:T(1024)} %param.28) | copy-start | bytes 24580
  97.1 145.1 %copy-start.2 = (f32[8192]{0:T(1024)S(1)}, f32[8192]{0:T(1024)}, u32[]{:S(2)}) copy-start(f32[8192]{0:T(1024)} %param.29) | copy-start | bytes 98308
  351.5 0.6 copy-start.4
  491.4 0.6 copy-start.1
Sparse Core Ops, SparseCore 0:
  635.5 117.6 all-reduce.1
where the time goes:
time: 762 us
  blocking collectives  467 us (61%)
  local copies, waits for them, and re-layouts  104 us (14%)
  waiting for transfers between devices  90.1 us (12%)
  matrix products  55.5 us (7%)
  other arithmetic  27.1 us (4%)
  between operations  14.5 us (2%)
    pmax x2, blocking collectives, merge_columns(): overall = lax.pmax(block_top, 'src')  126 us
    psum x2, blocking collectives, merge_columns(): return (overall, lax.psum(block_sum * jnp.exp(block_top - overall), 'src'))  117 us
    psum x1, waiting for transfers between devices, shards(): numerator, denominator = lax.psum((numerator, denominator), 'tgt')  90.1 us
    pmax x2, blocking collectives, merge_rows(): overall = lax.pmax(highest, 'tgt')  85.5 us
    psum x2, blocking collectives, merge_rows(): return (overall, lax.psum(totals * jnp.exp(highest - overall), 'tgt'))  56.9 us
    pmax x1, blocking collectives, shards(): overall = lax.pmax(local_top, 'tgt')  54.6 us
    dot_general x48, matrix products, pair_distance(): jnp.einsum('dr,dkc->krc', src_tile, tgt_chosen, preferred_element_type=jn...  45.6 us
    psum x1, blocking collectives, shards(): numerator, denominator = lax.psum((numerator, denominator), 'tgt')  27.6 us
  transfers between devices with their start and end apart: 1, of which 1 were waited for; matrix products, arithmetic and copies ran while one was open for 0% of the time, Pallas kernels for 0%

commit v1 on v0

--- a/solution.py
+++ b/solution.py
@@ -1,3 +1,4 @@
+import functools
 import jax
 import jax.numpy as jnp
 from jax import lax
@@ -9,6 +10,14 @@
 EPSILON = 0.1
 
 
+def things_feed(values, device_axis):
+    left_arr = jnp.sum(lax.all_gather(values, device_axis), 0)
+    return left_arr
+
+
+feed_counts = functools.partial(things_feed, device_axis="tgt")
+
+
 def pair_distance(src_tile, norm_tile, tgt_chosen, tgt_norm_chosen):
     products = jnp.einsum("dr,dkc->krc", src_tile, tgt_chosen, preferred_element_type=jnp.float32)
     return norm_tile[None, :, None] + tgt_norm_chosen[:, None, :] - 2.0 * products
@@ -16,7 +25,7 @@
 
 def merge_rows(highest, totals):
     overall = lax.pmax(highest, "tgt")
-    return (overall, lax.psum(totals * jnp.exp(highest - overall), "tgt"))
+    return (overall, feed_counts(totals * jnp.exp(highest - overall)))
 
 
 def merge_columns(block_top, block_sum):

time: 762 us -> 740 us (0.971)
  blocking collectives: 467 us -> 444 us
    psum x2 -> x0, blocking collectives: 56.9 us -> none  [merge_rows(): return (overall, lax.psum(totals * jnp.exp(highest - overall), 'tgt'))]
    all_gather x0 -> x2, blocking collectives: none -> 35.3 us  [things_feed(): left_arr = jnp.sum(lax.all_gather(values, device_axis), 0)]
where the time goes in v1:
time: 740 us; the launch traced here: 739 us
  blocking collectives  444 us (60%)
  local copies, waits for them, and re-layouts  104 us (14%)
  waiting for transfers between devices  90 us (12%)
  matrix products  55.5 us (8%)
  other arithmetic  27.1 us (4%)
  between operations  14.5 us (2%)
    pmax x2, blocking collectives, merge_columns(): overall = lax.pmax(block_top, 'src')  125 us
    psum x2, blocking collectives, merge_columns(): return (overall, lax.psum(block_sum * jnp.exp(block_top - overall), 'src'))  117 us
    psum x1, waiting for transfers between devices, shards(): numerator, denominator = lax.psum((numerator, denominator), 'tgt')  90 us
    pmax x2, blocking collectives, merge_rows(): overall = lax.pmax(highest, 'tgt')  85.4 us
    pmax x1, blocking collectives, shards(): overall = lax.pmax(local_top, 'tgt')  54.6 us
    dot_general x48, matrix products, pair_distance(): jnp.einsum('dr,dkc->krc', src_tile, tgt_chosen, preferred_element_type=jn...  45.6 us
    all_gather x2, blocking collectives, things_feed(): left_arr = jnp.sum(lax.all_gather(values, device_axis), 0)  35.3 us
    psum x1, blocking collectives, shards(): numerator, denominator = lax.psum((numerator, denominator), 'tgt')  27.6 us
  transfers between devices with their start and end apart: 1, of which 1 were waited for; matrix products, arithmetic and copies ran while one was open for 0% of the time, Pallas kernels for 0%

profile of v1, /device:TPU:1, one launch (start us, length us, event | category | flops | bytes accessed | tf_op | source)
XLA Modules:
  0.0 739.0 jit_solution(1789771213434570467)
XLA Ops:
  11.3 26.2 %while.70 = (s32[]{:T(128)}, f32[8,256]{1,0:T(8,128)S(1)}, f32[8,256]{1,0:T(8,128)S(1)}, pred[8,8]{1,0:T(8,128)(4,1)S(1)}, s32[8,8]{1,0:T(8,128)S(1)}, /*index=5...) while((s32[]{:T(128)}, f32[8,256]{1,0:T(8,128)S(1)}, ...), condition=%wide.region_5.8_spmd, body=%wide.region_2.7_spmd.sunk | while | flops 72487472 | bytes 5143929 | solution.py:85
  37.5 30.2 %pmax.35 = f32[2048]{0:T(1024)S(1)} all-reduce(f32[2048]{0:T(1024)S(1)} %bitcast.348), channel_id=1, replica_groups=mesh['src'=16,'tgt'=16] {'tgt'}, use_global_device_ids=true, to_apply=%region_6.9 | all-reduce | flops 2048 | bytes 16384 | tf_op jit(solution)/shard_map/pmax | solution.py:27
  67.8 18.5 %all-gather = f32[32768]{0:T(1024)S(1)} all-gather(f32[2048]{0:T(1024)S(1)} %exponential_multiply_fusion.3), channel_id=2, replica_groups=mesh['src'=16,'tgt'=16] {'tgt'}, dimensions={0}, use_global_device_ids=true | all-gather | bytes 139264 | tf_op jit(solution)/shard_map/all_gather | solution.py:14
  86.4 19.6 %while.71 = (s32[]{:T(128)}, f32[8,8,256]{2,1,0:T(8,128)S(1)}, f32[8,8,256]{2,1,0:T(8,128)S(1)}, pred[8,8]{1,0:T(8,128)(4,1)S(1)}, f32[8,256]{1,0:T(8,128)S(1)},...) while((s32[]{:T(128)}, f32[8,8,256]{2,1,0:T(8,128)S(1)}, ...), condition=%wide.region_11.14_spmd, body=%wide.region_8.13_spmd.sunk | while | flops 72481840 | bytes 5123405 | solution.py:100
  107.5 65.6 %pmax.36 = f32[8192]{0:T(1024)S(1)} all-reduce(f32[8192]{0:T(1024)S(1)} %bitcast.335), channel_id=1, replica_groups=mesh['src'=16,'tgt'=16] {'src'}, use_global_device_ids=true, to_apply=%region_13.16 | all-reduce | flops 8192 | bytes 65536 | tf_op jit(solution)/shard_map/pmax | solution.py:32
  173.1 58.0 %psum.28 = f32[8192]{0:T(1024)S(1)} all-reduce(f32[8192]{0:T(1024)S(1)} %exponential_multiply_fusion.1), channel_id=1, replica_groups=mesh['src'=16,'tgt'=16] {'src'}, use_global_device_ids=true, to_apply=%region_14.18 | all-reduce | flops 8192 | bytes 65536 | tf_op jit(solution)/shard_map/psum | solution.py:33
  231.2 26.1 %while.72 = (s32[]{:T(128)}, f32[8,256]{1,0:T(8,128)S(1)}, f32[8,256]{1,0:T(8,128)S(1)}, pred[8,8]{1,0:T(8,128)(4,1)S(1)}, s32[8,8]{1,0:T(8,128)S(1)}, /*index=5...) while((s32[]{:T(128)}, f32[8,256]{1,0:T(8,128)S(1)}, ...), condition=%wide.region_18.22_spmd, body=%wide.region_15.21_spmd.sunk | while | flops 72487472 | bytes 5111157 | solution.py:85
  257.4 55.2 %pmax.37 = f32[2048]{0:T(1024)S(1)} all-reduce(f32[2048]{0:T(1024)S(1)} %bitcast.350), channel_id=1, replica_groups=mesh['src'=16,'tgt'=16] {'tgt'}, use_global_device_ids=true, to_apply=%region_19.23 | all-reduce | flops 2048 | bytes 16384 | tf_op jit(solution)/shard_map/pmax | solution.py:27
  312.6 16.8 %all-gather.1 = f32[32768]{0:T(1024)S(1)} all-gather(f32[2048]{0:T(1024)S(1)} %exponential_multiply_fusion.2), channel_id=3, replica_groups=mesh['src'=16,'tgt'=16] {'tgt'}, dimensions={0}, use_global_device_ids=true | all-gather | bytes 139264 | tf_op jit(solution)/shard_map/all_gather | solution.py:14
  330.1 19.6 %while.73 = (s32[]{:T(128)}, f32[8,8,256]{2,1,0:T(8,128)S(1)}, f32[8,8,256]{2,1,0:T(8,128)S(1)}, pred[8,8]{1,0:T(8,128)(4,1)S(1)}, f32[8,256]{1,0:T(8,128)S(1)},...) while((s32[]{:T(128)}, f32[8,8,256]{2,1,0:T(8,128)S(1)}, ...), condition=%wide.region_24.28_spmd, body=%wide.region_21.27_spmd.sunk | while | flops 72481840 | bytes 5123405 | solution.py:100
  351.1 59.1 %pmax.38 = f32[8192]{0:T(1024)S(1)} all-reduce(f32[8192]{0:T(1024)S(1)} %bitcast.337), channel_id=1, replica_groups=mesh['src'=16,'tgt'=16] {'src'}, use_global_device_ids=true, to_apply=%region_26.30 | all-reduce | flops 8192 | bytes 65536 | tf_op jit(solution)/shard_map/pmax | solution.py:32
  410.3 58.6 %psum.29 = f32[8192]{0:T(1024)S(1)} all-reduce(f32[8192]{0:T(1024)S(1)} %exponential_multiply_fusion), channel_id=1, replica_groups=mesh['src'=16,'tgt'=16] {'src'}, use_global_device_ids=true, to_apply=%region_27.31 | all-reduce | flops 8192 | bytes 65536 | tf_op jit(solution)/shard_map/psum | solution.py:33
  469.5 24.2 %while.74 = (s32[]{:T(128)}, f32[8,256]{1,0:T(8,128)S(1)}, pred[8,8]{1,0:T(8,128)(4,1)S(1)}, s32[8,8]{1,0:T(8,128)S(1)}, f32[32,256]{1,0:T(8,128)S(1)}, /*index=...) while((s32[]{:T(128)}, f32[8,256]{1,0:T(8,128)S(1)}, ...), condition=%wide.region_30.34_spmd, body=%wide.region_28.33_spmd.sunk | while | flops 70914864 | bytes 912737 | solution.py:115
  493.7 3.2 copy.66
  496.9 2.9 copy.69
  499.9 55.7 %while.75 = (s32[]{:T(128)}, f32[8,256,128]{2,1,0:T(8,128)}, f32[8,256]{1,0:T(8,128)S(1)}, pred[8,8]{1,0:T(8,128)(4,1)S(1)}, s32[8,8]{1,0:T(8,128)S(1)}, /*index...) while((s32[]{:T(128)}, f32[8,256,128]{2,1,0:T(8,128)}, ...), condition=%wide.region_33.37_spmd, body=%wide.region_31.36_spmd.sunk | while | flops 207492928 | bytes 5770245 | solution.py:131
  510.1 2.2 gather_fusion.16
  524.0 2.2 gather_fusion.16
  531.0 2.2 gather_fusion.16
  538.0 2.2 gather_fusion.16
  555.6 54.6 %pmax.39 = f32[2048]{0:T(1024)S(1)} all-reduce(f32[2048]{0:T(1024)S(1)} %bitcast.346), channel_id=1, replica_groups=mesh['src'=16,'tgt'=16] {'tgt'}, use_global_device_ids=true, to_apply=%region_34.38 | all-reduce | flops 2048 | bytes 16384 | tf_op jit(solution)/shard_map/pmax | solution.py:137
  610.3 2.6 bitcast_multiply_fusion
  612.9 27.6 %psum.31 = f32[2048]{0:T(1024)S(1)} all-reduce(f32[2048]{0:T(1024)S(1)} %get-tuple-element.706), channel_id=1, replica_groups=mesh['src'=16,'tgt'=16] {'tgt'}, use_global_device_ids=true, to_apply=%region_36.40 | all-reduce | flops 2048 | bytes 16384 | tf_op jit(solution)/shard_map/psum | solution.py:141
  640.6 90.0 %all-reduce.2.cloned.1.call-done = f32[2048,128]{1,0:T(8,128)} async-done(((f32[2048,128]{1,0:T(8,128)}), f32[2048,128]{1,0:T(8,128)}) %all-reduce.2.cloned.1.call-update) | async-done | bytes 1048592 | tf_op jit(solution)/shard_map/psum | solution.py:141
  (647 shorter events, 169.1 us)
Async XLA Ops:
  7.2 3.8 copy-start
  7.2 723.4 %all-reduce.2.cloned.1.call-start = ((), (), s32[]{:S(2)}) async-start(), calls=%async_computation | async-start | bytes 2097152 | tf_op jit(solution)/shard_map/psum | solution.py:141
  8.1 3.1 copy-start.6
  8.1 3.2 copy-start.3
  11.3 75.0 %copy-start.5 = (f32[2048]{0:T(1024)S(1)}, f32[2048]{0:T(1024)}, u32[]{:S(2)}) copy-start(f32[2048]{0:T(1024)} %param.28) | copy-start | bytes 24580
  86.4 144.8 %copy-start.2 = (f32[8192]{0:T(1024)S(1)}, f32[8192]{0:T(1024)}, u32[]{:S(2)}) copy-start(f32[8192]{0:T(1024)} %param.29) | copy-start | bytes 98308
  329.5 0.6 copy-start.4
  468.9 0.6 copy-start.1
Sparse Core Ops, SparseCore 0:
  613.0 117.5 all-reduce.1
